TPU v7x, 32 devices: a whole 2x2x4 slice. The times are simulated.
32 devices in a mesh: dp: 8 (over y, x, core), tensor: 4 (over z).
Axes of the slice: x: 2, y: 2, z: 4, core: 2. Of those that a mesh axis runs over, the one named last changes fastest.
Arguments:
- tokens: bfloat16 [8192, 1536], P(('dp', 'tensor')), may hold values from -6 to 6
- first_gain: float32 [1536], replicated, may hold values from 0.25 to 1.75
- query_weight: bfloat16 [1536, 768], P(None, 'tensor'), may hold values from -0.0625 to 0.0625
- key_weight: bfloat16 [1536, 768], P(None, 'tensor'), may hold values from -0.0625 to 0.0625
- value_weight: bfloat16 [1536, 768], P(None, 'tensor'), may hold values from -0.15625 to 0.15625
- out_weight: bfloat16 [1536, 768], P(None, 'tensor'), may hold values from -0.875 to 0.875
- bucket_table: float32 [32, 12], P(None, 'tensor'), may hold values from -3 to 3
- second_gain: float32 [1536], replicated, may hold values from 0.25 to 1.75
- gate_weight: bfloat16 [1536, 3968], P(None, 'tensor'), may hold values from -0.15625 to 0.15625
- up_weight: bfloat16 [1536, 3968], P(None, 'tensor'), may hold values from -0.15625 to 0.15625
- down_weight: bfloat16 [1536, 3968], P(None, 'tensor'), may hold values from -0.09375 to 0.09375
- piece_start: int32 [8, 2], P('dp'), may hold values from 0 to 768, as said below
- bucket_index: int32 [2047], replicated, may hold values from 0 to 31, as said below
- cotangent: bfloat16 [8192, 1536], P(('dp', 'tensor')), may hold values from -6 to 6
Outputs:
- layer_out: bfloat16 [8192, 1536], P(('dp', 'tensor'))
- input_grad: bfloat16 [8192, 1536], P(('dp', 'tensor'))
- first_gain_grad: float32 [1536], replicated
- query_grad: float32 [1536, 768], P('dp', 'tensor')
- key_grad: float32 [1536, 768], P('dp', 'tensor')
- value_grad: float32 [1536, 768], P('dp', 'tensor')
- out_grad: float32 [1536, 768], P('dp', 'tensor')
- table_grad: float32 [32, 12], P(None, 'tensor')
- second_gain_grad: float32 [1536], replicated
- gate_grad: float32 [1536, 3968], P('dp', 'tensor')
- up_grad: float32 [1536, 3968], P('dp', 'tensor')
- down_grad: float32 [1536, 3968], P('dp', 'tensor')
Inputs may be any that keep to these rules, and one draw needn't show every extreme that they name: `piece_start`: piece p of a sequence lies within positions p * 512 to (p + 1) * 512 - 1, so pieces never intersect. bucket_index[d + 1023] is the bucket of key minus query position d: for d <= 0 it lies below 16 and equals |d| when |d| < 8; for d > 0 it is 16 plus the bucket that -d has, so it equals |d| + 32 // 2 when |d| < 8; it never falls as |d| grows on either side.
All inputs are finite; a program needn't handle non-finite values.
Results may differ from a plain program's by a relative error of at most 0.02.
Values may be sent and summed in bfloat16 or wider, within the bound.
A program may use at most 192 MiB of HBM per device.

v0:
```python
import jax
import jax.numpy as jnp
from jax import lax
from jax.sharding import PartitionSpec as P

NB = 32
LEN = 1024
QBLK = 512
PIECE = 256
NPIECE = 2
EPSILON = 1e-06
MASKED = -1000000000.0
HIGHEST = lax.Precision.HIGHEST


def normed(row_block, gain_vec):
    inv_rms = lax.rsqrt(jnp.mean(row_block * row_block, axis=-1, keepdims=True) + EPSILON)
    return row_block * inv_rms * gain_vec


def gelu_tanh(values):
    return jax.nn.gelu(values, approximate=True)


def piece_labels(starts_row, position):
    inside = (position[None, :] >= starts_row[:, None]) & (
        position[None, :] < starts_row[:, None] + PIECE
    )
    labels = jnp.arange(1, NPIECE + 1, dtype=jnp.int32)
    return jnp.sum(inside.astype(jnp.int32) * labels[:, None], axis=0) - 1


def bias_rows(distance_bias, query_start):
    width = QBLK + LEN - 1
    window = lax.dynamic_slice_in_dim(distance_bias, LEN - QBLK - query_start, width, 1)
    heads = window.shape[0]
    tiled = jnp.tile(window, (1, QBLK + 1))[:, : QBLK * (width + 1)]
    skewed = tiled.reshape(heads, QBLK, width + 1)[:, :, :LEN]
    return jnp.flip(skewed, axis=1)


def diagonal_sums(grad_block):
    width = QBLK + LEN - 1
    heads = grad_block.shape[0]
    flipped = jnp.flip(grad_block, axis=1)
    padded = jnp.pad(flipped, ((0, 0), (0, 0), (0, width + 1 - LEN)))
    flat = jnp.pad(padded.reshape(heads, QBLK * (width + 1)), ((0, 0), (0, LEN - 1)))
    return jnp.sum(flat.reshape(heads, QBLK + 1, width), axis=1)


def block_scores(query_block, key_seq, distance_bias, starts_row, query_start):
    query_pos = query_start + jnp.arange(QBLK, dtype=jnp.int32)
    key_pos = jnp.arange(LEN, dtype=jnp.int32)
    query_piece = piece_labels(starts_row, query_pos)
    key_piece = piece_labels(starts_row, key_pos)
    allowed = (key_pos[None, :] <= query_pos[:, None]) | (
        query_piece[:, None] == key_piece[None, :]
    ) & (query_piece[:, None] >= 0)
    raw_scores = jnp.einsum(
        "qhd,khd->hqk", query_block, key_seq, preferred_element_type=jnp.float32
    )
    return jnp.where(allowed[None], raw_scores + bias_rows(distance_bias, query_start), MASKED)


def locate(block_id):
    per_seq = LEN // QBLK
    sequence = block_id // per_seq
    query_start = block_id % per_seq * QBLK
    return (sequence, query_start, sequence * LEN + query_start)


def per_device(
    tokens,
    first_gain,
    query_weight,
    key_weight,
    value_weight,
    out_weight,
    bucket_table,
    second_gain,
    gate_weight,
    up_weight,
    down_weight,
    piece_start,
    bucket_index,
    cotangent,
):
    own_rows = tokens.shape[0]
    groups = piece_start.shape[0]
    all_rows = groups * LEN
    head_count = bucket_table.shape[1]
    inner_dev = query_weight.shape[1]
    head_dim = inner_dev // head_count
    block_count = all_rows // QBLK
    contract_cols = (((1,), (1,)), ((), ()))
    contract_rows = (((0,), (0,)), ((), ()))
    distance_hot = (bucket_index[:, None] == jnp.arange(NB, dtype=jnp.int32)[None, :]).astype(
        jnp.float32
    )
    distance_bias = jnp.dot(distance_hot, bucket_table, precision=HIGHEST).T
    inputs = tokens.astype(jnp.float32)
    norm_first = normed(inputs, first_gain).astype(jnp.bfloat16)
    first_all = lax.all_gather(norm_first, "tensor", axis=0, tiled=True)
    query_low = jnp.dot(first_all, query_weight, preferred_element_type=jnp.float32).astype(
        jnp.bfloat16
    )
    key_low = jnp.dot(first_all, key_weight, preferred_element_type=jnp.float32).astype(
        jnp.bfloat16
    )
    value_low = jnp.dot(first_all, value_weight, preferred_element_type=jnp.float32).astype(
        jnp.bfloat16
    )
    query_heads = query_low.reshape(all_rows, head_count, head_dim)
    key_heads = key_low.reshape(all_rows, head_count, head_dim)
    value_heads = value_low.reshape(all_rows, head_count, head_dim)

    def forward_block(block_id):
        sequence, query_start, row_start = locate(block_id)
        query_block = lax.dynamic_slice_in_dim(query_heads, row_start, QBLK, 0)
        scores = block_scores(
            query_block, key_heads, distance_bias, piece_start[sequence], query_start
        )
        peak = jnp.max(scores, axis=-1, keepdims=True)
        powered = jnp.exp(scores - peak)
        row_total = jnp.sum(powered, axis=-1, keepdims=True)
        softmax_low = (powered / row_total).astype(jnp.bfloat16)
        attended = jnp.einsum(
            "hqk,khd->qhd", softmax_low, value_heads, preferred_element_type=jnp.float32
        )
        return (attended.reshape(QBLK, inner_dev), (peak + jnp.log(row_total))[..., 0])

    attended, log_norms = lax.map(forward_block, jnp.arange(block_count, dtype=jnp.int32))
    attended_low = attended.reshape(all_rows, inner_dev).astype(jnp.bfloat16)
    picked = attended_low
    middle = inputs + lax.psum_scatter(
        lax.dot_general(
            picked, out_weight, contract_cols, preferred_element_type=jnp.float32
        ).astype(jnp.bfloat16),
        "tensor",
        scatter_dimension=0,
        tiled=True,
    ).astype(jnp.float32)
    norm_second = normed(middle, second_gain).astype(jnp.bfloat16)
    second_all = lax.all_gather(norm_second, "tensor", axis=0, tiled=True)
    gate_pre = jnp.dot(second_all, gate_weight, preferred_element_type=jnp.float32)
    up_proj = jnp.dot(second_all, up_weight, preferred_element_type=jnp.float32)
    activated, gelu_back = jax.vjp(gelu_tanh, gate_pre)
    hidden_low = (activated * up_proj).astype(jnp.bfloat16)
    picked = hidden_low
    layer_out = middle + lax.psum_scatter(
        lax.dot_general(
            picked, down_weight, contract_cols, preferred_element_type=jnp.float32
        ).astype(jnp.bfloat16),
        "tensor",
        scatter_dimension=0,
        tiled=True,
    ).astype(jnp.float32)
    grad_all = lax.all_gather(cotangent, "tensor", axis=0, tiled=True)
    down_grad = lax.dot_general(
        grad_all, hidden_low, contract_rows, preferred_element_type=jnp.float32
    )
    grad_hidden = jnp.dot(grad_all, down_weight, preferred_element_type=jnp.float32)
    (grad_act,) = gelu_back(grad_hidden * up_proj)
    grad_gate_low = grad_act.astype(jnp.bfloat16)
    grad_up_low = (grad_hidden * activated).astype(jnp.bfloat16)
    gate_grad = lax.dot_general(
        second_all, grad_gate_low, contract_rows, preferred_element_type=jnp.float32
    )
    up_grad = lax.dot_general(
        second_all, grad_up_low, contract_rows, preferred_element_type=jnp.float32
    )
    summed_rows = lax.dot_general(
        grad_gate_low, gate_weight, contract_cols, preferred_element_type=jnp.float32
    )
    grad_second = lax.psum_scatter(
        (
            summed_rows
            + lax.dot_general(
                grad_up_low, up_weight, contract_cols, preferred_element_type=jnp.float32
            )
        ).astype(jnp.bfloat16),
        "tensor",
        scatter_dimension=0,
        tiled=True,
    ).astype(jnp.float32)
    _, second_back = jax.vjp(normed, middle, second_gain)
    middle_part, second_gain_grad = second_back(grad_second)
    grad_middle = cotangent.astype(jnp.float32) + middle_part
    middle_all = lax.all_gather(grad_middle.astype(jnp.bfloat16), "tensor", axis=0, tiled=True)
    out_grad = lax.dot_general(
        middle_all, attended_low, contract_rows, preferred_element_type=jnp.float32
    )
    grad_attended = jnp.dot(middle_all, out_weight, preferred_element_type=jnp.float32).astype(
        jnp.bfloat16
    )
    grad_attended = grad_attended.reshape(all_rows, head_count, head_dim)

    def backward_block(block_id, running):
        grad_query, grad_key, grad_value, grad_distance = running
        sequence, query_start, row_start = locate(block_id)
        query_block = lax.dynamic_slice_in_dim(query_heads, row_start, QBLK, 0)
        scores = block_scores(
            query_block, key_heads, distance_bias, piece_start[sequence], query_start
        )
        softmax_rows = jnp.exp(scores - log_norms[block_id][..., None])
        grad_block = lax.dynamic_slice_in_dim(grad_attended, row_start, QBLK, 0)
        grad_probs = jnp.einsum(
            "qhd,khd->hqk", grad_block, value_heads, preferred_element_type=jnp.float32
        )
        weighted = jnp.sum(softmax_rows * grad_probs, axis=-1, keepdims=True)
        grad_scores = (softmax_rows * (grad_probs - weighted)).astype(jnp.bfloat16)
        query_part = jnp.einsum(
            "hqk,khd->qhd", grad_scores, key_heads, preferred_element_type=jnp.float32
        )
        key_part = jnp.einsum(
            "hqk,qhd->khd", grad_scores, query_block, preferred_element_type=jnp.float32
        )
        value_part = jnp.einsum(
            "hqk,qhd->khd",
            softmax_rows.astype(jnp.bfloat16),
            grad_block,
            preferred_element_type=jnp.float32,
        )
        grad_query = lax.dynamic_update_slice_in_dim(grad_query, query_part, row_start, 0)
        grad_key = grad_key + key_part
        grad_value = grad_value + value_part
        diag_part = diagonal_sums(grad_scores.astype(jnp.float32))
        width = QBLK + LEN - 1
        diag_from = LEN - QBLK - query_start
        current = lax.dynamic_slice_in_dim(grad_distance, diag_from, width, 1)
        grad_distance = lax.dynamic_update_slice_in_dim(
            grad_distance, current + diag_part, diag_from, 1
        )
        return (grad_query, grad_key, grad_value, grad_distance)

    zero_heads = jnp.zeros((all_rows, head_count, head_dim), jnp.float32)
    zero_distance = jnp.zeros((head_count, 2 * LEN - 1), jnp.float32)
    grad_query, grad_key, grad_value, grad_distance = lax.fori_loop(
        0, block_count, backward_block, (zero_heads, zero_heads, zero_heads, zero_distance)
    )
    table_grad = jnp.dot(distance_hot.T, grad_distance.T, precision=HIGHEST)
    grad_query_low = grad_query.reshape(all_rows, inner_dev).astype(jnp.bfloat16)
    grad_key_low = grad_key.reshape(all_rows, inner_dev).astype(jnp.bfloat16)
    grad_value_low = grad_value.reshape(all_rows, inner_dev).astype(jnp.bfloat16)
    query_grad = lax.dot_general(
        first_all, grad_query_low, contract_rows, preferred_element_type=jnp.float32
    )
    key_grad = lax.dot_general(
        first_all, grad_key_low, contract_rows, preferred_element_type=jnp.float32
    )
    value_grad = lax.dot_general(
        first_all, grad_value_low, contract_rows, preferred_element_type=jnp.float32
    )
    summed_rows = jnp.zeros(
        (lax.axis_size("tensor") * own_rows, query_weight.shape[0]), jnp.float32
    )
    for grad_low, weight in (
        (grad_query_low, query_weight),
        (grad_key_low, key_weight),
        (grad_value_low, value_weight),
    ):
        picked = grad_low
        summed_rows = summed_rows + lax.dot_general(
            picked, weight, contract_cols, preferred_element_type=jnp.float32
        )
    grad_first = lax.psum_scatter(
        summed_rows.astype(jnp.bfloat16), "tensor", scatter_dimension=0, tiled=True
    ).astype(jnp.float32)
    _, first_back = jax.vjp(normed, inputs, first_gain)
    input_part, first_gain_grad = first_back(grad_first)
    input_grad = grad_middle + input_part
    query_grad, key_grad, value_grad, out_grad, gate_grad, up_grad, down_grad = (
        lax.psum_scatter(query_grad, "dp", scatter_dimension=0, tiled=True),
        lax.psum_scatter(key_grad, "dp", scatter_dimension=0, tiled=True),
        lax.psum_scatter(value_grad, "dp", scatter_dimension=0, tiled=True),
        lax.psum_scatter(out_grad, "dp", scatter_dimension=0, tiled=True),
        lax.psum_scatter(gate_grad, "dp", scatter_dimension=0, tiled=True),
        lax.psum_scatter(up_grad, "dp", scatter_dimension=0, tiled=True),
        lax.psum_scatter(down_grad, "dp", scatter_dimension=0, tiled=True),
    )
    table_grad = lax.psum(table_grad, "dp")
    first_gain_grad, second_gain_grad = lax.psum(
        (first_gain_grad, second_gain_grad), ("dp", "tensor")
    )
    return (
        layer_out.astype(jnp.bfloat16),
        input_grad.astype(jnp.bfloat16),
        first_gain_grad,
        query_grad,
        key_grad,
        value_grad,
        out_grad,
        table_grad,
        second_gain_grad,
        gate_grad,
        up_grad,
        down_grad,
    )


def solution(mesh):
    return jax.shard_map(
        per_device,
        mesh=mesh,
        in_specs=(
            P(("dp", "tensor"), None),
            P(),
            P(None, "tensor"),
            P(None, "tensor"),
            P(None, "tensor"),
            P(None, "tensor"),
            P(None, "tensor"),
            P(),
            P(None, "tensor"),
            P(None, "tensor"),
            P(None, "tensor"),
            P("dp", None),
            P(),
            P(("dp", "tensor"), None),
        ),
        out_specs=(
            P(("dp", "tensor"), None),
            P(("dp", "tensor"), None),
            P(),
            P("dp", "tensor"),
            P("dp", "tensor"),
            P("dp", "tensor"),
            P("dp", "tensor"),
            P(None, "tensor"),
            P(),
            P("dp", "tensor"),
            P("dp", "tensor"),
            P("dp", "tensor"),
        ),
        check_vma=False,
    )
```

profile of v0, /device:TPU:0, one launch (start us, length us, event | category | flops | bytes accessed | tf_op | source)
XLA Modules:
  0.0 1671.4 jit_solution(16654163404661405045)
XLA Ops:
  13.0 65.6 %all-gather.5.cloned.1.call-done = bf16[1024,1536]{1,0:T(8,128)(2,1)} async-done(((bf16[256,1536]{1,0:T(8,128)(2,1)}), bf16[1024,1536]{1,0:T(8,128)(2,1)}) %all-gather.5.cloned.1.call-update) | async-done | bytes 3145744 | tf_op jit(solution)/shard_map/all_gather | solution.py:103
  85.8 241.3 %while.38 = (s32[]{:T(128)}, bf16[2,512,192]{1,2,0:T(8,128)(2,1)}, f32[2,3,512]{2,1,0:T(4,128)}, s32[2]{0:T(128)S(1)}, s32[1,2]{1,0:T(1,128)}, /*index=5*/bf16[1...) while((s32[]{:T(128)}, bf16[2,512,192]{1,2,0:T(8,128)(2,1)}, ...), condition=%wide.region_6.7_spmd, body=%wide.region_1.6_spmd.sunk | while | flops 417348640 | bytes 142808624 | solution.py:132
  148.9 48.5 %rev.35 = f32[3,512,1024]{2,1,0:T(8,128)} reverse(f32[3,512,1024]{2,1,0:T(8,128)} %slice.47), dimensions={1} | reverse | bytes 12582912 | tf_op jit(solution)/shard_map/while/body/eval_jaxpr/jit(_flip)/rev | solution.py:39
  269.2 48.5 %rev.35 = f32[3,512,1024]{2,1,0:T(8,128)} reverse(f32[3,512,1024]{2,1,0:T(8,128)} %slice.47), dimensions={1} | reverse | bytes 12582912 | tf_op jit(solution)/shard_map/while/body/eval_jaxpr/jit(_flip)/rev | solution.py:39
  332.7 59.0 %reduce-scatter.14.cloned.1.call-done = bf16[256,1536]{1,0:T(8,128)(2,1)} async-done(((bf16[1024,1536]{1,0:T(8,128)(2,1)}), bf16[256,1536]{1,0:T(8,128)(2,1)}) %reduce-scatter.14.cloned.1.call-update) | async-done | bytes 786448 | tf_op jit(solution)/shard_map/reduce_scatter | solution.py:135
  396.6 63.1 %all-gather.7.cloned.1.call-done = bf16[1024,1536]{1,0:T(8,128)(2,1)} async-done(((bf16[256,1536]{1,0:T(8,128)(2,1)}), bf16[1024,1536]{1,0:T(8,128)(2,1)}) %all-gather.7.cloned.1.call-update) | async-done | bytes 3145744 | tf_op jit(solution)/shard_map/all_gather | solution.py:144
  472.9 50.4 %all-gather.9.cloned.1.call-done = bf16[1024,1536]{1,0:T(8,128)(2,1)} async-done(((bf16[256,1536]{1,0:T(8,128)(2,1)}), bf16[1024,1536]{1,0:T(8,128)(2,1)}) %all-gather.9.cloned.1.call-update) | async-done | bytes 3145744 | tf_op jit(solution)/shard_map/all_gather | solution.py:158
  542.5 59.0 %reduce-scatter.18.cloned.1.call-done = bf16[256,1536]{1,0:T(8,128)(2,1)} async-done(((bf16[1024,1536]{1,0:T(8,128)(2,1)}), bf16[256,1536]{1,0:T(8,128)(2,1)}) %reduce-scatter.18.cloned.1.call-update) | async-done | bytes 786448 | tf_op jit(solution)/shard_map/reduce_scatter | solution.py:175
  607.9 63.6 %all-gather.11.cloned.1.call-done = bf16[1024,1536]{1,0:T(8,128)(2,1)} async-done(((bf16[256,1536]{1,0:T(8,128)(2,1)}), bf16[1024,1536]{1,0:T(8,128)(2,1)}) %all-gather.11.cloned.1.call-update) | async-done | bytes 3145744 | tf_op jit(solution)/shard_map/all_gather | solution.py:189
  676.2 489.1 %while.39 = (s32[]{:T(128)}, bf16[1024,3,64]{0,2,1:T(8,128)(2,1)}, f32[1024,3,64]{0,2,1:T(8,128)}, f32[1024,3,64]{0,2,1:T(8,128)}, f32[3,2047]{1,0:T(4,128)S(1)}...) while((s32[]{:T(128)}, bf16[1024,3,64]{0,2,1:T(8,128)(2,1)}, ...), condition=%wide.region_17.18_spmd.clone, body=%wide.region_12.17_spmd.clone.sunk | while | flops 1026050048 | bytes 305763776 | solution.py:238
  742.1 48.5 %rev.36 = f32[3,512,1024]{2,1,0:T(8,128)} reverse(f32[3,512,1024]{2,1,0:T(8,128)} %slice.49), dimensions={1} | reverse | bytes 12582912 | tf_op jit(solution)/shard_map/while/body/eval_jaxpr/jit(_flip)/rev | solution.py:39
  806.1 46.0 %rev.37 = f32[3,512,1024]{2,1,0:T(8,128)} reverse(bf16[3,512,1024]{2,1,0:T(8,128)(2,1)} %copy-done.1), dimensions={1} | reverse | bytes 9437184 | tf_op jit(solution)/shard_map/while/body/eval_jaxpr/jit(_flip)/rev | solution.py:45
  856.1 19.9 %copy.48 = f32[1,3,512,1536]{3,1,2,0:T(4,128)S(1)} copy(f32[1,3,512,1536]{3,2,1,0:T(8,128)S(1)} %pad_bitcast_fusion.2) | data formatting | bytes 18874368 | tf_op jit(solution)/shard_map/while
  982.1 48.5 %rev.36 = f32[3,512,1024]{2,1,0:T(8,128)} reverse(f32[3,512,1024]{2,1,0:T(8,128)} %slice.49), dimensions={1} | reverse | bytes 12582912 | tf_op jit(solution)/shard_map/while/body/eval_jaxpr/jit(_flip)/rev | solution.py:39
  1047.1 46.0 %rev.37 = f32[3,512,1024]{2,1,0:T(8,128)} reverse(bf16[3,512,1024]{2,1,0:T(8,128)(2,1)} %copy-done.1), dimensions={1} | reverse | bytes 9437184 | tf_op jit(solution)/shard_map/while/body/eval_jaxpr/jit(_flip)/rev | solution.py:45
  1097.2 19.9 %copy.48 = f32[1,3,512,1536]{3,1,2,0:T(4,128)S(1)} copy(f32[1,3,512,1536]{3,2,1,0:T(8,128)S(1)} %pad_bitcast_fusion.2) | data formatting | bytes 18874368 | tf_op jit(solution)/shard_map/while
  1248.3 43.6 %all-reduce.2 = (f32[1536]{0:T(1024)}, f32[1536]{0:T(1024)}) all-reduce(f32[1536]{0:T(1024)S(1)} %get-tuple-element.593, f32[1536]{0:T(1024)S(1)} %copy-done.23), channel_id=1, replica_groups=mesh['dp'=8,'tensor'=4] {'dp','tensor'}, use_global_device_ids=true, to_apply=%region_21.22 | all-reduce | flops 3072 | bytes 24576 | tf_op jit(solution)/shard_map/psum | solution.py:282
  1301.4 61.1 %reduce-scatter.34.cloned.1.call-done = f32[192,992]{1,0:T(8,128)} async-done(((f32[1536,992]{1,0:T(8,128)}), f32[192,992]{1,0:T(8,128)}) %reduce-scatter.34.cloned.1.call-update) | async-done | bytes 761872
  1362.5 65.9 %reduce-scatter.32.cloned.1.call-done = f32[192,992]{1,0:T(8,128)} async-done(((f32[1536,992]{1,0:T(8,128)}), f32[192,992]{1,0:T(8,128)}) %reduce-scatter.32.cloned.1.call-update) | async-done | bytes 761872 | tf_op jit(solution)/shard_map/reduce_scatter | solution.py:278
  1428.4 65.7 %reduce-scatter.30.cloned.1.call-done = f32[192,992]{1,0:T(8,128)} async-done(((f32[1536,992]{1,0:T(8,128)}), f32[192,992]{1,0:T(8,128)}) %reduce-scatter.30.cloned.1.call-update) | async-done | bytes 761872 | tf_op jit(solution)/shard_map/reduce_scatter | solution.py:277
  1494.2 42.5 %reduce-scatter.28.cloned.1.call-done = f32[192,192]{1,0:T(8,128)} async-done(((f32[1536,192]{1,0:T(8,128)}), f32[192,192]{1,0:T(8,128)}) %reduce-scatter.28.cloned.1.call-update) | async-done | bytes 147472 | tf_op jit(solution)/shard_map/reduce_scatter | solution.py:276
  1536.7 42.7 %reduce-scatter.26.cloned.1.call-done = f32[192,192]{1,0:T(8,128)} async-done(((f32[1536,192]{1,0:T(8,128)}), f32[192,192]{1,0:T(8,128)}) %reduce-scatter.26.cloned.1.call-update) | async-done | bytes 147472 | tf_op jit(solution)/shard_map/reduce_scatter | solution.py:275
  1579.4 42.5 %reduce-scatter.22.cloned.1.call-done = f32[192,192]{1,0:T(8,128)} async-done(((f32[1536,192]{1,0:T(8,128)}), f32[192,192]{1,0:T(8,128)}) %reduce-scatter.22.cloned.1.call-update) | async-done | bytes 147472 | tf_op jit(solution)/shard_map/reduce_scatter | solution.py:273
  1621.9 42.5 %reduce-scatter.24.cloned.1.call-done = f32[192,192]{1,0:T(8,128)} async-done(((f32[1536,192]{1,0:T(8,128)}), f32[192,192]{1,0:T(8,128)}) %reduce-scatter.24.cloned.1.call-update) | async-done | bytes 147472 | tf_op jit(solution)/shard_map/reduce_scatter | solution.py:274
  (283 shorter events, 549.1 us)
Async XLA Ops:
  7.2 516.1 %copy-start = (bf16[1536,992]{0,1:T(8,128)(2,1)S(1)}, bf16[1536,992]{0,1:T(8,128)(2,1)}, u32[]{:S(2)}) copy-start(bf16[1536,992]{0,1:T(8,128)(2,1)} %param.28) | copy-start | bytes 9142276
  7.2 71.3 %all-gather.5.cloned.1.call-start = ((), (), s32[]{:S(2)}) async-start(), calls=%async_computation.11 | async-start | bytes 3932160 | tf_op jit(solution)/shard_map/all_gather | solution.py:103
  12.2 379.5 %reduce-scatter.14.cloned.1.call-start = ((), (), s32[]{:S(2)}) async-start(), calls=%async_computation.12 | async-start | bytes 3932160 | tf_op jit(solution)/shard_map/reduce_scatter | solution.py:135
  332.6 60.8 %copy-start.20 = (f32[1536]{0:T(1024)S(1)}, f32[1536]{0:T(1024)}, u32[]{:S(2)}) copy-start(f32[1536]{0:T(1024)} %param.25) | copy-start | bytes 18436
  332.6 127.0 %all-gather.7.cloned.1.call-start = ((), (), s32[]{:S(2)}) async-start(), calls=%async_computation.13 | async-start | bytes 3932160 | tf_op jit(solution)/shard_map/all_gather | solution.py:144
  393.4 211.0 %copy-start.24 = (f32[256]{0:T(256)}, f32[256]{0:T(256)S(1)}, u32[]{:S(2)}) copy-start(f32[256]{0:T(256)S(1)} %fusion.53) | copy-start | bytes 3076
  396.0 127.3 %all-gather.9.cloned.1.call-start = ((), (), s32[]{:S(2)}) async-start(), calls=%async_computation.15 | async-start | bytes 3932160 | tf_op jit(solution)/shard_map/all_gather | solution.py:158
  396.6 204.9 %reduce-scatter.18.cloned.1.call-start = ((), (), s32[]{:S(2)}) async-start(), calls=%async_computation.16 | async-start | bytes 3932160 | tf_op jit(solution)/shard_map/reduce_scatter | solution.py:175
  542.4 129.0 %all-gather.11.cloned.1.call-start = ((), (), s32[]{:S(2)}) async-start(), calls=%async_computation.17 | async-start | bytes 3932160 | tf_op jit(solution)/shard_map/all_gather | solution.py:189
  604.4 71.0 %copy-start.30 = (f32[256]{0:T(256)}, f32[256]{0:T(256)S(1)}, u32[]{:S(2)}) copy-start(f32[256]{0:T(256)S(1)} %multiply_multiply_fusion.4) | copy-start | bytes 3076
  607.8 638.4 %reduce-scatter.20.cloned.1.call-start = ((), (), s32[]{:S(2)}) async-start(), calls=%async_computation.18 | async-start | bytes 3932160 | tf_op jit(solution)/shard_map/reduce_scatter | solution.py:266
  1174.1 122.7 %reduce-scatter.16.cloned.1.call-start = ((), (), s32[]{:S(2)}) async-start(), calls=%async_computation.14 | async-start | bytes 3932160 | tf_op jit(solution)/shard_map/reduce_scatter | solution.py:150
  1180.7 181.8 %reduce-scatter.34.cloned.1.call-start = ((), (), s32[]{:S(2)}) async-start(), calls=%async_computation.25 | async-start | bytes 7077888
  1195.8 232.7 %reduce-scatter.32.cloned.1.call-start = ((), (), s32[]{:S(2)}) async-start(), calls=%async_computation.24 | async-start | bytes 7077888 | tf_op jit(solution)/shard_map/reduce_scatter | solution.py:278
  1204.5 289.7 %reduce-scatter.30.cloned.1.call-start = ((), (), s32[]{:S(2)}) async-start(), calls=%async_computation.23 | async-start | bytes 7077888 | tf_op jit(solution)/shard_map/reduce_scatter | solution.py:277
  1213.4 323.3 %reduce-scatter.28.cloned.1.call-start = ((), (), s32[]{:S(2)}) async-start(), calls=%async_computation.22 | async-start | bytes 1769472 | tf_op jit(solution)/shard_map/reduce_scatter | solution.py:276
  1218.5 360.9 %reduce-scatter.26.cloned.1.call-start = ((), (), s32[]{:S(2)}) async-start(), calls=%async_computation.21 | async-start | bytes 1769472 | tf_op jit(solution)/shard_map/reduce_scatter | solution.py:275
  1222.8 399.1 %reduce-scatter.22.cloned.1.call-start = ((), (), s32[]{:S(2)}) async-start(), calls=%async_computation.19 | async-start | bytes 1769472 | tf_op jit(solution)/shard_map/reduce_scatter | solution.py:273
  1227.0 19.2 %copy-start.22 = (f32[1536]{0:T(1024)S(1)}, f32[1536]{0:T(1024)}, u32[]{:S(2)}) copy-start(f32[1536]{0:T(1024)} %param.19) | copy-start | bytes 18436
  1227.0 437.4 %reduce-scatter.24.cloned.1.call-start = ((), (), s32[]{:S(2)}) async-start(), calls=%async_computation.20 | async-start | bytes 1769472 | tf_op jit(solution)/shard_map/reduce_scatter | solution.py:274
  1231.3 60.6 %copy-start.29 = (f32[256]{0:T(256)S(1)}, f32[256]{0:T(256)}, u32[]{:S(2)}) copy-start(f32[256]{0:T(256)} %copy-done.28) | copy-start | bytes 3076
  1231.3 65.5 %copy-start.21 = (f32[1536]{0:T(1024)S(1)}, f32[1536]{0:T(1024)}, u32[]{:S(2)}) copy-start(f32[1536]{0:T(1024)} %param.25) | copy-start | bytes 18436
  1231.3 65.5 %copy-start.25 = (f32[256]{0:T(256)S(1)}, f32[256]{0:T(256)}, u32[]{:S(2)}) copy-start(f32[256]{0:T(256)} %copy-done.24) | copy-start | bytes 3076
  1231.3 65.4 %copy-start.31 = (f32[256]{0:T(256)S(1)}, f32[256]{0:T(256)}, u32[]{:S(2)}) copy-start(f32[256]{0:T(256)} %copy-done.30) | copy-start | bytes 3076
  (43 other events, 157.7 us)
Sparse Core Ops, SparseCore 0:
  12.3 66.1 all-gather.4
  332.7 58.8 reduce-scatter.13
  396.1 63.5 all-gather.6
  461.1 62.1 all-gather.8
  542.6 58.8 reduce-scatter.17
  607.9 63.5 all-gather.10
  1174.2 58.8 reduce-scatter.19
  1235.4 61.3 reduce-scatter.15
  1300.7 61.7 reduce-scatter.33
  1366.7 61.7 reduce-scatter.31
  1432.4 61.7 reduce-scatter.29
  1498.3 38.4 reduce-scatter.27
  1540.9 38.4 reduce-scatter.25
  1583.5 38.4 reduce-scatter.21
  1626.0 38.4 reduce-scatter.23
where the time goes:
time: 1700 us; the launch traced here: 1670 us
  waiting for transfers between devices  729 us (43%)
  local copies, waits for them, and re-layouts  650 us (38%)
  matrix products  145 us (9%)
  other arithmetic  58.7 us (3%)
  blocking collectives  57.9 us (3%)
    rev x4, local copies, waits for them, and re-layouts, bias_rows(): return jnp.flip(skewed, axis=1)  194 us
    while x54, local copies, waits for them, and re-layouts  172 us
    rev x2, local copies, waits for them, and re-layouts, diagonal_sums(): flipped = jnp.flip(grad_block, axis=1)  92 us
    another operation x8, local copies, waits for them, and re-layouts, bias_rows(): tiled = jnp.tile(window, (1, QBLK + 1))[:, :QBLK * (width + 1)]  75.5 us
    reduce_scatter x1, waiting for transfers between devices, per_device(): lax.psum_scatter(up_grad, 'dp', scatter_dimension=0, tiled=True)  65.9 us
    reduce_scatter x1, waiting for transfers between devices, per_device(): lax.psum_scatter(gate_grad, 'dp', scatter_dimension=0, tiled=True)  65.7 us
    all_gather x1, waiting for transfers between devices, per_device(): first_all = lax.all_gather(norm_first, 'tensor', axis=0, tiled=True)  65.6 us
    all_gather x1, waiting for transfers between devices, per_device(): lax.all_gather(grad_middle.astype(jnp.bfloat16), 'tensor', axis=0, tiled=...  63.6 us
  transfers between devices with their start and end apart: 15, of which 14 were waited for; matrix products, arithmetic and copies ran while one was open for 5% of the time, Pallas kernels for 0%

commit v1 on v0

--- a/solution.py
+++ b/solution.py
@@ -155,7 +155,14 @@
         scatter_dimension=0,
         tiled=True,
     ).astype(jnp.float32)
-    grad_all = lax.all_gather(cotangent, "tensor", axis=0, tiled=True)
+    peers = lax.axis_size("tensor")
+    right = [(i, (i + 1) % peers) for i in range(peers)]
+    parts = [cotangent]
+    for reach in range(1, peers):
+        parts = [lax.ppermute(parts[0], "tensor", right), *parts]
+    whole = jnp.concatenate(parts, axis=0)
+    shift = (lax.axis_index("tensor") + 1) * parts[-1].shape[0]
+    grad_all = jnp.roll(whole, shift, axis=0)
     down_grad = lax.dot_general(
         grad_all, hidden_low, contract_rows, preferred_element_type=jnp.float32
     )

time: 1700 us -> 1700 us (level)
  starting transfers between devices: 0.87 us -> 25.1 us
  waiting for transfers between devices: 729 us -> 705 us
    ppermute x0 -> x3, waiting for transfers between devices: none -> 81 us  [per_device(): parts = [lax.ppermute(parts[0], 'tensor', right), *parts]]
    all_gather x1, waiting for transfers between devices: 63.1 us -> 0.01 us  [per_device(): second_all = lax.all_gather(norm_second, 'tensor', axis=0, tiled=True)]
    unnamed x16 -> x14, waiting for transfers between devices: 61.8 us -> 0.23 us
    reduce_scatter x0 -> x1, waiting for transfers between devices: none -> 61.2 us  [per_device(): lax.psum_scatter(down_grad, 'dp', scatter_dimension=0, tiled=True)]
    all_gather x1 -> x0, waiting for transfers between devices: 50.4 us -> none  [per_device(): grad_all = lax.all_gather(cotangent, 'tensor', axis=0, tiled=True)]
    ppermute x0 -> x3, starting transfers between devices: none -> 24.2 us  [per_device(): parts = [lax.ppermute(parts[0], 'tensor', right), *parts]]
  transfers between devices with their start and end apart: 15 -> 17, of which waited for: 14 -> 15; matrix products, arithmetic and copies ran while one was open for 5% -> 4% of each run, Pallas kernels for 0% -> 0%
where the time goes in v1:
time: 1700 us; the launch traced here: 1670 us
  waiting for transfers between devices  705 us (41%)
  local copies, waits for them, and re-layouts  656 us (39%)
  matrix products  141 us (8%)
  other arithmetic  59 us (3%)
  blocking collectives  56 us (3%)
  starting transfers between devices  25.1 us (1%)
    rev x4, local copies, waits for them, and re-layouts, bias_rows(): return jnp.flip(skewed, axis=1)  194 us
    while x54, local copies, waits for them, and re-layouts  172 us
    rev x2, local copies, waits for them, and re-layouts, diagonal_sums(): flipped = jnp.flip(grad_block, axis=1)  91.9 us
    ppermute x3, waiting for transfers between devices, per_device(): parts = [lax.ppermute(parts[0], 'tensor', right), *parts]  81 us
    another operation x8, local copies, waits for them, and re-layouts, bias_rows(): tiled = jnp.tile(window, (1, QBLK + 1))[:, :QBLK * (width + 1)]  75.5 us
    reduce_scatter x1, waiting for transfers between devices, per_device(): lax.psum_scatter(up_grad, 'dp', scatter_dimension=0, tiled=True)  66.1 us
    reduce_scatter x1, waiting for transfers between devices, per_device(): lax.psum_scatter(gate_grad, 'dp', scatter_dimension=0, tiled=True)  65.6 us
    all_gather x1, waiting for transfers between devices, per_device(): first_all = lax.all_gather(norm_first, 'tensor', axis=0, tiled=True)  65.6 us
  transfers between devices with their start and end apart: 17, of which 15 were waited for; matrix products, arithmetic and copies ran while one was open for 4% of the time, Pallas kernels for 0%

profile of v1, /device:TPU:0, one launch (start us, length us, event | category | flops | bytes accessed | tf_op | source)
XLA Modules:
  0.0 1672.7 jit_solution(3331185454591609009)
XLA Ops:
  12.9 65.6 %all-gather.4.cloned.1.call-done = bf16[1024,1536]{1,0:T(8,128)(2,1)} async-done(((bf16[256,1536]{1,0:T(8,128)(2,1)}), bf16[1024,1536]{1,0:T(8,128)(2,1)}) %all-gather.4.cloned.1.call-update) | async-done | bytes 3145744 | tf_op jit(solution)/shard_map/all_gather | solution.py:103
  85.7 241.1 %while.38 = (s32[]{:T(128)}, bf16[2,512,192]{1,2,0:T(8,128)(2,1)}, f32[2,3,512]{2,1,0:T(4,128)}, s32[2]{0:T(128)S(1)}, s32[1,2]{1,0:T(1,128)}, /*index=5*/bf16[1...) while((s32[]{:T(128)}, bf16[2,512,192]{1,2,0:T(8,128)(2,1)}, ...), condition=%wide.region_6.7_spmd, body=%wide.region_1.6_spmd.sunk | while | flops 417348640 | bytes 142808624 | solution.py:132
  148.8 48.4 %rev.35 = f32[3,512,1024]{2,1,0:T(8,128)} reverse(f32[3,512,1024]{2,1,0:T(8,128)} %slice.47), dimensions={1} | reverse | bytes 12582912 | tf_op jit(solution)/shard_map/while/body/eval_jaxpr/jit(_flip)/rev | solution.py:39
  269.0 48.4 %rev.35 = f32[3,512,1024]{2,1,0:T(8,128)} reverse(f32[3,512,1024]{2,1,0:T(8,128)} %slice.47), dimensions={1} | reverse | bytes 12582912 | tf_op jit(solution)/shard_map/while/body/eval_jaxpr/jit(_flip)/rev | solution.py:39
  332.5 59.0 %reduce-scatter.12.cloned.1.call-done = bf16[256,1536]{1,0:T(8,128)(2,1)} async-done(((bf16[1024,1536]{1,0:T(8,128)(2,1)}), bf16[256,1536]{1,0:T(8,128)(2,1)}) %reduce-scatter.12.cloned.1.call-update) | async-done | bytes 786448 | tf_op jit(solution)/shard_map/reduce_scatter | solution.py:135
  396.9 29.9 %collective-permute-done = bf16[256,1536]{1,0:T(8,128)(2,1)S(1)} collective-permute-done((bf16[256,1536]{1,0:T(8,128)(2,1)}, bf16[256,1536]{1,0:T(8,128)(2,1)S(1)}, u32[]{:S(2)}, u32[]{:S(2)}) %collective-permute-start) | collective-permute-done | bytes 786464 | tf_op jit(solution)/shard_map/ppermute | solution.py:162
  438.6 32.5 %collective-permute-done.1 = bf16[256,1536]{1,0:T(8,128)(2,1)} collective-permute-done((bf16[256,1536]{1,0:T(8,128)(2,1)S(1)}, bf16[256,1536]{1,0:T(8,128)(2,1)}, u32[]{:S(2)}, u32[]{:S(2)}) %collective-permute-start.1) | collective-permute-done | bytes 786464 | tf_op jit(solution)/shard_map/ppermute | solution.py:162
  541.9 59.9 %reduce-scatter.16.cloned.1.call-done = bf16[256,1536]{1,0:T(8,128)(2,1)} async-done(((bf16[1024,1536]{1,0:T(8,128)(2,1)}), bf16[256,1536]{1,0:T(8,128)(2,1)}) %reduce-scatter.16.cloned.1.call-update) | async-done | bytes 786448 | tf_op jit(solution)/shard_map/reduce_scatter | solution.py:182
  608.2 63.6 %all-gather.8.cloned.1.call-done = bf16[1024,1536]{1,0:T(8,128)(2,1)} async-done(((bf16[256,1536]{1,0:T(8,128)(2,1)}), bf16[1024,1536]{1,0:T(8,128)(2,1)}) %all-gather.8.cloned.1.call-update) | async-done | bytes 3145744 | tf_op jit(solution)/shard_map/all_gather | solution.py:196
  676.6 489.7 %while.39 = (s32[]{:T(128)}, bf16[1024,3,64]{0,2,1:T(8,128)(2,1)}, f32[1024,3,64]{0,2,1:T(8,128)}, f32[1024,3,64]{0,2,1:T(8,128)}, f32[3,2047]{1,0:T(4,128)S(1)}...) while((s32[]{:T(128)}, bf16[1024,3,64]{0,2,1:T(8,128)(2,1)}, ...), condition=%wide.region_17.18_spmd.clone, body=%wide.region_12.17_spmd.clone.sunk | while | flops 1026050048 | bytes 305763776 | solution.py:245
  742.5 48.4 %rev.36 = f32[3,512,1024]{2,1,0:T(8,128)} reverse(f32[3,512,1024]{2,1,0:T(8,128)} %slice.49), dimensions={1} | reverse | bytes 12582912 | tf_op jit(solution)/shard_map/while/body/eval_jaxpr/jit(_flip)/rev | solution.py:39
  806.4 45.9 %rev.37 = f32[3,512,1024]{2,1,0:T(8,128)} reverse(bf16[3,512,1024]{2,1,0:T(8,128)(2,1)} %copy-done.1), dimensions={1} | reverse | bytes 9437184 | tf_op jit(solution)/shard_map/while/body/eval_jaxpr/jit(_flip)/rev | solution.py:45
  856.3 19.9 %copy.41 = f32[1,3,512,1536]{3,1,2,0:T(4,128)S(1)} copy(f32[1,3,512,1536]{3,2,1,0:T(8,128)S(1)} %pad_bitcast_fusion.2) | data formatting | bytes 18874368 | tf_op jit(solution)/shard_map/while
  982.3 48.4 %rev.36 = f32[3,512,1024]{2,1,0:T(8,128)} reverse(f32[3,512,1024]{2,1,0:T(8,128)} %slice.49), dimensions={1} | reverse | bytes 12582912 | tf_op jit(solution)/shard_map/while/body/eval_jaxpr/jit(_flip)/rev | solution.py:39
  1047.4 45.9 %rev.37 = f32[3,512,1024]{2,1,0:T(8,128)} reverse(bf16[3,512,1024]{2,1,0:T(8,128)(2,1)} %copy-done.1), dimensions={1} | reverse | bytes 9437184 | tf_op jit(solution)/shard_map/while/body/eval_jaxpr/jit(_flip)/rev | solution.py:45
  1097.3 19.9 %copy.41 = f32[1,3,512,1536]{3,1,2,0:T(4,128)S(1)} copy(f32[1,3,512,1536]{3,2,1,0:T(8,128)S(1)} %pad_bitcast_fusion.2) | data formatting | bytes 18874368 | tf_op jit(solution)/shard_map/while
  1243.7 41.6 %all-reduce.2 = (f32[1536]{0:T(1024)}, f32[1536]{0:T(1024)}) all-reduce(f32[1536]{0:T(1024)S(1)} %get-tuple-element.545, f32[1536]{0:T(1024)S(1)} %copy-done.26), channel_id=1, replica_groups=mesh['dp'=8,'tensor'=4] {'dp','tensor'}, use_global_device_ids=true, to_apply=%region_21.22 | all-reduce | flops 3072 | bytes 24576 | tf_op jit(solution)/shard_map/psum | solution.py:289
  1302.3 61.2 %reduce-scatter.32.cloned.1.call-done = f32[192,992]{1,0:T(8,128)} async-done(((f32[1536,992]{1,0:T(8,128)}), f32[192,992]{1,0:T(8,128)}) %reduce-scatter.32.cloned.1.call-update) | async-done | bytes 761872 | tf_op jit(solution)/shard_map/reduce_scatter | solution.py:286
  1363.5 66.1 %reduce-scatter.30.cloned.1.call-done = f32[192,992]{1,0:T(8,128)} async-done(((f32[1536,992]{1,0:T(8,128)}), f32[192,992]{1,0:T(8,128)}) %reduce-scatter.30.cloned.1.call-update) | async-done | bytes 761872 | tf_op jit(solution)/shard_map/reduce_scatter | solution.py:285
  1429.6 65.6 %reduce-scatter.28.cloned.1.call-done = f32[192,992]{1,0:T(8,128)} async-done(((f32[1536,992]{1,0:T(8,128)}), f32[192,992]{1,0:T(8,128)}) %reduce-scatter.28.cloned.1.call-update) | async-done | bytes 761872 | tf_op jit(solution)/shard_map/reduce_scatter | solution.py:284
  1495.2 42.7 %reduce-scatter.26.cloned.1.call-done = f32[192,192]{1,0:T(8,128)} async-done(((f32[1536,192]{1,0:T(8,128)}), f32[192,192]{1,0:T(8,128)}) %reduce-scatter.26.cloned.1.call-update) | async-done | bytes 147472 | tf_op jit(solution)/shard_map/reduce_scatter | solution.py:283
  1537.9 42.6 %reduce-scatter.24.cloned.1.call-done = f32[192,192]{1,0:T(8,128)} async-done(((f32[1536,192]{1,0:T(8,128)}), f32[192,192]{1,0:T(8,128)}) %reduce-scatter.24.cloned.1.call-update) | async-done | bytes 147472 | tf_op jit(solution)/shard_map/reduce_scatter | solution.py:282
  1580.4 42.7 %reduce-scatter.20.cloned.1.call-done = f32[192,192]{1,0:T(8,128)} async-done(((f32[1536,192]{1,0:T(8,128)}), f32[192,192]{1,0:T(8,128)}) %reduce-scatter.20.cloned.1.call-update) | async-done | bytes 147472 | tf_op jit(solution)/shard_map/reduce_scatter | solution.py:280
  1623.1 42.6 %reduce-scatter.22.cloned.1.call-done = f32[192,192]{1,0:T(8,128)} async-done(((f32[1536,192]{1,0:T(8,128)}), f32[192,192]{1,0:T(8,128)}) %reduce-scatter.22.cloned.1.call-update) | async-done | bytes 147472 | tf_op jit(solution)/shard_map/reduce_scatter | solution.py:281
  (297 shorter events, 601.6 us)
Async XLA Ops:
  7.2 516.6 %copy-start = (bf16[1536,992]{0,1:T(8,128)(2,1)S(1)}, bf16[1536,992]{0,1:T(8,128)(2,1)}, u32[]{:S(2)}) copy-start(bf16[1536,992]{0,1:T(8,128)(2,1)} %param.28) | copy-start | bytes 9142276
  7.2 71.3 %all-gather.4.cloned.1.call-start = ((), (), s32[]{:S(2)}) async-start(), calls=%async_computation.11 | async-start | bytes 3932160 | tf_op jit(solution)/shard_map/all_gather | solution.py:103
  12.1 379.3 %reduce-scatter.12.cloned.1.call-start = ((), (), s32[]{:S(2)}) async-start(), calls=%async_computation.12 | async-start | bytes 3932160 | tf_op jit(solution)/shard_map/reduce_scatter | solution.py:135
  332.4 60.8 %copy-start.23 = (f32[1536]{0:T(1024)S(1)}, f32[1536]{0:T(1024)}, u32[]{:S(2)}) copy-start(f32[1536]{0:T(1024)} %param.25) | copy-start | bytes 18436
  332.4 181.7 %all-gather.6.cloned.1.call-start = ((), (), s32[]{:S(2)}) async-start(), calls=%async_computation.13 | async-start | bytes 3932160 | tf_op jit(solution)/shard_map/all_gather | solution.py:144
  393.2 211.6 %copy-start.27 = (f32[256]{0:T(256)}, f32[256]{0:T(256)S(1)}, u32[]{:S(2)}) copy-start(f32[256]{0:T(256)S(1)} %fusion.57) | copy-start | bytes 3076
  395.8 206.1 %reduce-scatter.16.cloned.1.call-start = ((), (), s32[]{:S(2)}) async-start(), calls=%async_computation.15 | async-start | bytes 3932160 | tf_op jit(solution)/shard_map/reduce_scatter | solution.py:182
  395.8 31.0 %collective-permute-start = (bf16[256,1536]{1,0:T(8,128)(2,1)}, bf16[256,1536]{1,0:T(8,128)(2,1)S(1)}, u32[]{:S(2)}, u32[]{:S(2)}) collective-permute-start(bf16[256,1536]{1,0:T(8,128)(2,1)} %param.31), channel_id=1, source_target_pairs={{0,1},{1,2},{2,3},{3,0},{4,5},{5,6},{6,7},{7,4},{8,9},{9,10},{10,1... | collective-permute-start | bytes 2359304 | tf_op jit(solution)/shard_map/ppermute | solution.py:162
  427.7 43.4 %collective-permute-start.1 = (bf16[256,1536]{1,0:T(8,128)(2,1)S(1)}, bf16[256,1536]{1,0:T(8,128)(2,1)}, u32[]{:S(2)}, u32[]{:S(2)}) collective-permute-start(bf16[256,1536]{1,0:T(8,128)(2,1)S(1)} %collective-permute-done), channel_id=1, source_target_pairs={{0,1},{1,2},{2,3},{3,0},{4,5},{5,6},{6,7},{7,4},{8,9},{9,10},{10,1... | collective-permute-start | bytes 2359304 | tf_op jit(solution)/shard_map/ppermute | solution.py:162
  471.0 30.9 %collective-permute-start.2 = (bf16[256,1536]{1,0:T(8,128)(2,1)}, bf16[256,1536]{1,0:T(8,128)(2,1)}, u32[]{:S(2)}, u32[]{:S(2)}) collective-permute-start(bf16[256,1536]{1,0:T(8,128)(2,1)} %collective-permute-done.1), channel_id=1, source_target_pairs={{0,1},{1,2},{2,3},{3,0},{4,5},{5,6},{6,7},{7,4},{8,9},{9,10},{10,1... | collective-permute-start | bytes 2359304 | tf_op jit(solution)/shard_map/ppermute | solution.py:162
  541.9 129.9 %all-gather.8.cloned.1.call-start = ((), (), s32[]{:S(2)}) async-start(), calls=%async_computation.16 | async-start | bytes 3932160 | tf_op jit(solution)/shard_map/all_gather | solution.py:196
  604.8 71.0 %copy-start.33 = (f32[256]{0:T(256)}, f32[256]{0:T(256)S(1)}, u32[]{:S(2)}) copy-start(f32[256]{0:T(256)S(1)} %multiply_multiply_fusion.4) | copy-start | bytes 3076
  608.2 633.2 %reduce-scatter.18.cloned.1.call-start = ((), (), s32[]{:S(2)}) async-start(), calls=%async_computation.17 | async-start | bytes 3932160 | tf_op jit(solution)/shard_map/reduce_scatter | solution.py:273
  1175.0 122.6 %reduce-scatter.14.cloned.1.call-start = ((), (), s32[]{:S(2)}) async-start(), calls=%async_computation.14 | async-start | bytes 3932160 | tf_op jit(solution)/shard_map/reduce_scatter | solution.py:150
  1181.7 181.8 %reduce-scatter.32.cloned.1.call-start = ((), (), s32[]{:S(2)}) async-start(), calls=%async_computation.24 | async-start | bytes 7077888 | tf_op jit(solution)/shard_map/reduce_scatter | solution.py:286
  1190.5 239.1 %reduce-scatter.30.cloned.1.call-start = ((), (), s32[]{:S(2)}) async-start(), calls=%async_computation.23 | async-start | bytes 7077888 | tf_op jit(solution)/shard_map/reduce_scatter | solution.py:285
  1199.2 295.9 %reduce-scatter.28.cloned.1.call-start = ((), (), s32[]{:S(2)}) async-start(), calls=%async_computation.22 | async-start | bytes 7077888 | tf_op jit(solution)/shard_map/reduce_scatter | solution.py:284
  1208.2 329.7 %reduce-scatter.26.cloned.1.call-start = ((), (), s32[]{:S(2)}) async-start(), calls=%async_computation.21 | async-start | bytes 1769472 | tf_op jit(solution)/shard_map/reduce_scatter | solution.py:283
  1213.4 367.1 %reduce-scatter.24.cloned.1.call-start = ((), (), s32[]{:S(2)}) async-start(), calls=%async_computation.20 | async-start | bytes 1769472 | tf_op jit(solution)/shard_map/reduce_scatter | solution.py:282
  1217.8 405.4 %reduce-scatter.20.cloned.1.call-start = ((), (), s32[]{:S(2)}) async-start(), calls=%async_computation.18 | async-start | bytes 1769472 | tf_op jit(solution)/shard_map/reduce_scatter | solution.py:280
  1221.9 443.7 %reduce-scatter.22.cloned.1.call-start = ((), (), s32[]{:S(2)}) async-start(), calls=%async_computation.19 | async-start | bytes 1769472 | tf_op jit(solution)/shard_map/reduce_scatter | solution.py:281
  1226.2 71.4 %copy-start.24 = (f32[1536]{0:T(1024)S(1)}, f32[1536]{0:T(1024)}, u32[]{:S(2)}) copy-start(f32[1536]{0:T(1024)} %param.25) | copy-start | bytes 18436
  1226.2 71.4 %copy-start.28 = (f32[256]{0:T(256)S(1)}, f32[256]{0:T(256)}, u32[]{:S(2)}) copy-start(f32[256]{0:T(256)} %copy-done.27) | copy-start | bytes 3076
  1226.2 71.4 %copy-start.34 = (f32[256]{0:T(256)S(1)}, f32[256]{0:T(256)}, u32[]{:S(2)}) copy-start(f32[256]{0:T(256)} %copy-done.33) | copy-start | bytes 3076
  (47 other events, 269.8 us)
Sparse Core Ops, SparseCore 0:
  12.3 66.1 all-gather.3
  332.5 58.8 reduce-scatter.11
  395.9 89.0 all-gather.5
  542.0 59.8 reduce-scatter.15
  608.3 63.5 all-gather.7
  1175.1 58.8 reduce-scatter.17
  1236.4 61.2 reduce-scatter.13
  1301.6 61.8 reduce-scatter.31
  1367.8 61.7 reduce-scatter.29
  1433.4 61.7 reduce-scatter.27
  1499.4 38.4 reduce-scatter.25
  1541.9 38.4 reduce-scatter.23
  1584.7 38.4 reduce-scatter.19
  1627.2 38.4 reduce-scatter.21
